TPU v7x, 32 devices: a whole 2x2x4 slice. The times are simulated.
32 devices in a mesh: tm: 16 (over z, y, core), head: 2 (over x).
Axes of the slice: x: 2, y: 2, z: 4, core: 2. Of those that a mesh axis runs over, the one named last changes fastest.
Arguments:
- queries: bfloat16 [4096, 2048], P('tm', 'head'), may hold values from -48 to 48
- keys: bfloat16 [4096, 2048], P('tm', 'head'), may hold values from -6 to 6
- values_in: bfloat16 [4096, 2048], P('tm', 'head'), may hold values from -32 to 32
- teacher: bfloat16 [4096, 2048], P('tm', 'head'), may hold values from -6 to 6
- gain: float32 [2048], P('head'), may hold values from 0.25 to 1.75
- conv_weight: float32 [4, 2048], P(None, 'head'), may hold values from -3 to 3
- block_bits: int32 [32, 6], P('tm'), may hold values from 0 to 1, as said below
- mask_pos: int32 [32, 64], P('tm'), may hold values from 0 to 127, as said below
Outputs:
- query_grad: bfloat16 [4096, 2048], P('tm', 'head')
- key_grad: bfloat16 [4096, 2048], P('tm', 'head')
- value_grad: bfloat16 [4096, 2048], P('tm', 'head')
- conv_grad: float32 [4, 2048], P(None, 'head')
Inputs may be any that keep to these rules, and one draw needn't show every extreme that they name: `block_bits`: column 0 of every row is 1. `mask_pos`: each row names 64 different positions.
All inputs are finite; a program needn't handle non-finite values.
Results may differ from a plain program's by a relative error of at most 0.0095.
Values may be sent and summed in bfloat16 or wider, within the bound.
A program may use at most 64 MiB of HBM per device.

v0:
```python
from functools import reduce

import jax
import jax.numpy as jnp
from jax import lax
from jax.sharding import PartitionSpec as P

D = 2048
HD = 128
BLK = 128
REACH = 3


NEG_FILL = -1e30
NORM_EPS = 1e-06


def from_behind(block, axis, distance):
    devices = range(lax.axis_size(axis))
    route = [(i - distance, i) for i in devices if i - distance in devices]
    return lax.ppermute(block, axis, route)


def split_heads(array):
    return array.reshape(array.shape[0], array.shape[1] // HD, HD)


def pair_mask(block_bits, device, distance, row_count):
    per_device = row_count // BLK
    window = block_bits.shape[1]
    block_index = jnp.arange(per_device, dtype=jnp.int32)
    relative = distance * per_device + block_index[:, None] - block_index[None, :]
    one_hot = relative[:, :, None] == jnp.arange(window, dtype=jnp.int32)[None, None, :]
    picked_bits = jnp.sum(jnp.where(one_hot, block_bits[:, None, :], 0), axis=2)
    coarse_mask = (picked_bits > 0) & (relative < window)
    fine_mask = jnp.repeat(jnp.repeat(coarse_mask, BLK, axis=0), BLK, axis=1)
    offsets = jnp.arange(row_count, dtype=jnp.int32)
    causal = (distance > 0) | (offsets[None, :] <= offsets[:, None])
    return fine_mask & causal & (device >= distance)


def body(queries, keys, values_in, teacher, gain, conv_weight, block_bits, mask_pos):
    row_count, channels = queries.shape
    tap_count = conv_weight.shape[0]
    rim_rows = tap_count - 1
    device = lax.axis_index("tm")
    score_scale = HD ** (-0.5)
    prior = from_behind(values_in[row_count - rim_rows :], "tm", 1)
    extended = jnp.concatenate([prior, values_in], 0).astype(jnp.float32)
    conv_sum = jnp.zeros((row_count, channels), jnp.float32)
    for tap_index in range(tap_count):
        conv_sum = (
            conv_sum
            + conv_weight[tap_index]
            * extended[rim_rows - tap_index : rim_rows - tap_index + row_count]
        )
    values = conv_sum.astype(jnp.bfloat16)
    blocks = [(keys, values)]
    for distance in range(1, REACH + 1):
        moved_keys, moved_values = from_behind((keys, values), "tm", distance)
        blocks.append((moved_keys, moved_values))
    heads_query = split_heads(queries)
    pair_masks = [
        pair_mask(block_bits, device, distance, row_count) for distance in range(REACH + 1)
    ]
    scores = []
    for distance in range(REACH + 1):
        raw_scores = (
            jnp.einsum(
                "thd,uhd->htu",
                heads_query,
                split_heads(blocks[distance][0]),
                preferred_element_type=jnp.float32,
            )
            * score_scale
        )
        scores.append(jnp.where(pair_masks[distance][None], raw_scores, NEG_FILL))
    row_peak = reduce(jnp.maximum, [jnp.max(block_scores, axis=2) for block_scores in scores])
    expos = [
        jnp.where(pair_masks[distance][None], jnp.exp(scores[distance] - row_peak[..., None]), 0.0)
        for distance in range(REACH + 1)
    ]
    row_total = reduce(jnp.add, [jnp.sum(expo_block, axis=2) for expo_block in expos])
    probs = [expo_block / row_total[..., None] for expo_block in expos]
    attended = jnp.zeros((row_count, channels // HD, HD), jnp.float32)
    for distance in range(REACH + 1):
        weights = probs[distance].astype(jnp.bfloat16)
        attended = attended + jnp.einsum(
            "htu,uhd->thd",
            weights,
            split_heads(blocks[distance][1]),
            preferred_element_type=jnp.float32,
        )
    flattened = attended.reshape(row_count, channels)
    squares = lax.psum(jnp.sum(flattened * flattened, axis=1), "head")
    inverse = lax.rsqrt(squares / D + NORM_EPS)
    prediction = flattened * inverse[:, None] * gain
    position = jnp.arange(row_count, dtype=jnp.int32) % BLK
    chosen = jnp.any(jnp.repeat(mask_pos, BLK, axis=0) == position[:, None], axis=1)
    residual = jnp.where(chosen[:, None], prediction - teacher.astype(jnp.float32), 0.0)
    scaled = residual * gain
    cross_term = lax.psum(jnp.sum(scaled * flattened, axis=1), "head")
    out_grad = (
        inverse[:, None] * scaled - flattened * (inverse**3 * cross_term / D)[:, None]
    ).astype(jnp.bfloat16)
    heads_grad = split_heads(out_grad)
    delta = jnp.sum(heads_grad.astype(jnp.float32) * attended, axis=2).T
    query_acc = jnp.zeros((row_count, channels // HD, HD), jnp.float32)
    partials = []
    for distance in range(REACH + 1):
        block_keys, block_values = blocks[distance]
        prob = probs[distance]
        prob_grad = jnp.einsum(
            "thd,uhd->htu",
            heads_grad,
            split_heads(block_values),
            preferred_element_type=jnp.float32,
        )
        score_grad = (prob * (prob_grad - delta[:, :, None])).astype(jnp.bfloat16)
        query_acc = (
            query_acc
            + jnp.einsum(
                "htu,uhd->thd",
                score_grad,
                split_heads(block_keys),
                preferred_element_type=jnp.float32,
            )
            * score_scale
        )
        key_part = (
            jnp.einsum("htu,thd->uhd", score_grad, heads_query, preferred_element_type=jnp.float32)
            * score_scale
        )
        value_part = jnp.einsum(
            "htu,thd->uhd",
            prob.astype(jnp.bfloat16),
            heads_grad,
            preferred_element_type=jnp.float32,
        )
        partials.append(
            (key_part.reshape(row_count, channels), value_part.reshape(row_count, channels))
        )
    key_acc, value_acc = partials[0]
    for distance in range(1, REACH + 1):
        back_keys, back_values = (
            from_behind(partials[distance][0].astype(jnp.bfloat16), "tm", -distance).astype(
                jnp.float32
            ),
            from_behind(partials[distance][1].astype(jnp.bfloat16), "tm", -distance).astype(
                jnp.float32
            ),
        )
        key_acc = key_acc + back_keys
        value_acc = value_acc + back_values
    following = from_behind(value_acc[:rim_rows], "tm", -1)
    padded_acc = jnp.concatenate([value_acc, following], 0)
    value_sum = jnp.zeros((row_count, channels), jnp.float32)
    for tap_index in range(tap_count):
        value_sum = (
            value_sum + conv_weight[tap_index] * padded_acc[tap_index : tap_index + row_count]
        )
    local_taps = jnp.stack(
        [
            jnp.sum(
                value_acc * extended[rim_rows - tap_index : rim_rows - tap_index + row_count],
                axis=0,
            )
            for tap_index in range(tap_count)
        ]
    )
    conv_grad = lax.psum(local_taps, "tm")
    return (
        query_acc.reshape(row_count, channels).astype(jnp.bfloat16),
        key_acc.astype(jnp.bfloat16),
        value_sum.astype(jnp.bfloat16),
        conv_grad,
    )


def solution(mesh):
    placed = (
        P("tm", "head"),
        P("tm", "head"),
        P("tm", "head"),
        P("tm", "head"),
        P("head"),
        P(None, "head"),
        P("tm", None),
        P("tm", None),
    )
    return jax.shard_map(
        body,
        mesh=mesh,
        in_specs=placed,
        out_specs=(P("tm", "head"), P("tm", "head"), P("tm", "head"), P(None, "head")),
        check_vma=False,
    )
```

profile of v0, /device:TPU:0, one launch (start us, length us, event | category | flops | bytes accessed | tf_op | source)
XLA Modules:
  0.0 256.2 jit_solution(13179985974177373972)
XLA Ops:
  1.9 4.3 %collective-permute-start.2 = (bf16[256,1024]{0,1:T(8,128)(2,1)S(1)}, bf16[256,1024]{0,1:T(8,128)(2,1)S(1)}, u32[]{:S(2)}, u32[]{:S(2)}) collective-permute-start(bf16[256,1024]{0,1:T(8,128)(2,1)S(1)} %copy.234), channel_id=1, source_target_pairs={{0,6},{2,8},{4,10},{6,12},{8,14},{10,16},{12,18},{14,20},{16,22},{... | collective-permute-start | bytes 1572872 | tf_op jit(solution)/shard_map/ppermute | solution.py:21
  6.2 4.3 %collective-permute-start.1 = (bf16[256,1024]{0,1:T(8,128)(2,1)S(1)}, bf16[256,1024]{0,1:T(8,128)(2,1)}, u32[]{:S(2)}, u32[]{:S(2)}) collective-permute-start(bf16[256,1024]{0,1:T(8,128)(2,1)S(1)} %copy.234), channel_id=1, source_target_pairs={{0,4},{2,6},{4,8},{6,10},{8,12},{10,14},{12,16},{14,18},{16,20},{1... | collective-permute-start | bytes 1572872 | tf_op jit(solution)/shard_map/ppermute | solution.py:21
  10.5 2.3 collective-permute-start
  13.6 2.2 collective-permute-start.3
  22.6 13.8 %collective-permute-start.5 = (bf16[256,1024]{1,0:T(8,128)(2,1)}, bf16[256,1024]{1,0:T(8,128)(2,1)}, u32[]{:S(2)}, u32[]{:S(2)}) collective-permute-start(bf16[256,1024]{1,0:T(8,128)(2,1)} %add_convert_fusion.1), channel_id=1, source_target_pairs={{0,4},{2,6},{4,8},{6,10},{8,12},{10,14},{12,16},{14,18},{16,20},{1... | collective-permute-start | bytes 1572872 | tf_op jit(solution)/shard_map/ppermute | solution.py:21
  36.4 7.2 %collective-permute-start.4 = (bf16[256,1024]{1,0:T(8,128)(2,1)}, bf16[256,1024]{1,0:T(8,128)(2,1)}, u32[]{:S(2)}, u32[]{:S(2)}) collective-permute-start(bf16[256,1024]{1,0:T(8,128)(2,1)} %add_convert_fusion.1), channel_id=1, source_target_pairs={{0,2},{2,4},{4,6},{6,8},{8,10},{10,12},{12,14},{14,16},{16,18},{18... | collective-permute-start | bytes 1572872 | tf_op jit(solution)/shard_map/ppermute | solution.py:21
  44.2 4.4 %collective-permute-start.6 = (bf16[256,1024]{1,0:T(8,128)(2,1)}, bf16[256,1024]{1,0:T(8,128)(2,1)}, u32[]{:S(2)}, u32[]{:S(2)}) collective-permute-start(bf16[256,1024]{1,0:T(8,128)(2,1)} %add_convert_fusion.1), channel_id=1, source_target_pairs={{0,6},{2,8},{4,10},{6,12},{8,14},{10,16},{12,18},{14,20},{16,22},{... | collective-permute-start | bytes 1572872 | tf_op jit(solution)/shard_map/ppermute | solution.py:21
  55.8 3.7 %collective-permute-done.6 = bf16[256,1024]{1,0:T(8,128)(2,1)} collective-permute-done((bf16[256,1024]{1,0:T(8,128)(2,1)}, bf16[256,1024]{1,0:T(8,128)(2,1)}, u32[]{:S(2)}, u32[]{:S(2)}) %collective-permute-start.6) | collective-permute-done | bytes 524320 | tf_op jit(solution)/shard_map/ppermute | solution.py:21
  60.7 3.6 %fusion.34 = f32[8,128,256]{2,1,0:T(8,128)} fusion(bf16[256,8,128]{0,2,1:T(8,128)(2,1)S(1)} %bitcast.178, f32[8,256,256]{1,2,0:T(8,128)} %copy-done.6, f32[8,256]{1,0:T(8,128)S(1)} %add_add_fusion, f32[8,256]{1,0:T(8,128)S(1)} %maximum_maximum_fusion, pred[256,256]{0,1:T(8,128)(4,1)S(1)} %bitcast.175), kind=kOutput, calls=%fused_computation.73 | convolution fusion | flops 137363456 | bytes 3751936 | tf_op jit(solution)/shard_map/htu,uhd->thd/dot_general | solution.py:88
  65.6 3.8 %convolution_add_fusion.3 = f32[8,128,256]{2,1,0:T(8,128)} fusion(f32[8,128,256]{2,1,0:T(8,128)} %fusion.30, bf16[256,8,128]{0,2,1:T(8,128)(2,1)S(1)} %bitcast.180, f32[8,256,256]{1,2,0:T(8,128)} %copy-done.2, f32[8,256]{1,0:T(8,128)S(1)} %add_add_fusion, f32[8,256]{1,0:T(8,128)S(1)} %maximum_maximum_fusion, pred[256,256]{0,1:T(8,128)(4,1)S(1)} %bitcast.165), kind=kOutput, calls=%fused_computation.36 | convolution fusion | flops 137625600 | bytes 4800512 | tf_op jit(solution)/shard_map/htu,uhd->thd/dot_general | solution.py:88
  70.7 4.2 %fusion.28 = (f32[256]{0:T(256)S(1)}, f32[8,128,256]{2,1,0:T(8,128)}) fusion(f32[8,128,256]{2,1,0:T(8,128)} %fusion.34, f32[8,128,256]{2,1,0:T(8,128)} %convolution_add_fusion.3, bf16[256,8,128]{0,2,1:T(8,128)(2,1)S(1)} %bitcast.182, f32[8,256]{1,0:T(8,128)S(1)} %add_add_fusion, f32[8,256]{1,0:T(8,128)S(1)} %maximum_maximum_fusion, ...), kind=kOutput, calls=%fused_computation.56 | convolution fusion | flops 138411776 | bytes 5850112 | tf_op jit(solution)/shard_map/htu,uhd->thd/dot_general | solution.py:88
  74.9 5.1 %psum.21 = f32[256]{0:T(256)S(1)} all-reduce(f32[256]{0:T(256)S(1)} %get-tuple-element.41), channel_id=1, replica_groups=mesh['tm'=16,'head'=2] {'head'}, use_global_device_ids=true, to_apply=%region_13.14 | all-reduce | flops 256 | bytes 2048 | tf_op jit(solution)/shard_map/psum | solution.py:95
  83.1 5.1 %psum.22 = f32[256]{0:T(256)S(1)} all-reduce(f32[256]{0:T(256)S(1)} %multiply_reduce_fusion.4), channel_id=1, replica_groups=mesh['tm'=16,'head'=2] {'head'}, use_global_device_ids=true, to_apply=%region_16.17 | all-reduce | flops 256 | bytes 2048 | tf_op jit(solution)/shard_map/psum | solution.py:102
  88.2 2.2 subtract_convert_fusion
  93.2 3.4 %convolution_convert_fusion.2 = bf16[8,128,256]{2,1,0:T(8,128)(2,1)} fusion(bf16[256,8,128]{0,2,1:T(8,128)(2,1)S(1)} %bitcast.150, f32[8,256,256]{1,2,0:T(8,128)} %copy-done.2, f32[8,256]{1,0:T(8,128)S(1)} %add_add_fusion, f32[8,256]{1,0:T(8,128)S(1)} %maximum_maximum_fusion, pred[256,256]{0,1:T(8,128)(4,1)S(1)} %bitcast.166), kind=kOutput, calls=%fused_computation.43 | convolution fusion | flops 137625600 | bytes 3227648 | tf_op jit(solution)/shard_map/htu,thd->uhd/dot_general | solution.py:134
  96.6 2.1 multiply_convert_fusion.2
  116.6 2.5 copy.198
  122.3 2.6 %fusion.17 = bf16[8,256,128]{1,2,0:T(8,128)(2,1)} fusion(bf16[8,256,256]{1,2,0:T(8,128)(2,1)} %multiply_convert_fusion, bf16[256,8,128]{0,2,1:T(8,128)(2,1)S(1)} %bitcast.140), kind=kOutput, calls=%fused_computation.39 | convolution fusion | flops 134742016 | bytes 2097152 | tf_op jit(solution)/shard_map/htu,thd->uhd/dot_general | solution.py:131
  126.1 2.2 copy.191
  139.1 33.0 %collective-permute-done.12 = bf16[256,1024]{1,0:T(8,128)(2,1)S(1)} collective-permute-done((bf16[256,1024]{1,0:T(8,128)(2,1)}, bf16[256,1024]{1,0:T(8,128)(2,1)S(1)}, u32[]{:S(2)}, u32[]{:S(2)}) %collective-permute-start.12) | collective-permute-done | bytes 524320 | tf_op jit(solution)/shard_map/ppermute | solution.py:21
  173.6 2.1 fusion.18
  177.8 2.4 multiply_reduce_fusion.3
  181.5 2.5 add_convert_fusion
  184.0 70.9 %psum.23 = f32[4,1024]{1,0:T(4,128)} all-reduce(f32[4,1024]{1,0:T(4,128)S(1)} %pad_maximum_fusion.1), channel_id=1, replica_groups=mesh['tm'=16,'head'=2] {'tm'}, use_global_device_ids=true, to_apply=%region_22.23 | all-reduce | flops 4096 | bytes 32768 | tf_op jit(solution)/shard_map/psum | solution.py:171
  (155 shorter events, 64.7 us)
Async XLA Ops:
  1.9 49.3 %collective-permute-start.2 = (bf16[256,1024]{0,1:T(8,128)(2,1)S(1)}, bf16[256,1024]{0,1:T(8,128)(2,1)S(1)}, u32[]{:S(2)}, u32[]{:S(2)}) collective-permute-start(bf16[256,1024]{0,1:T(8,128)(2,1)S(1)} %copy.234), channel_id=1, source_target_pairs={{0,6},{2,8},{4,10},{6,12},{8,14},{10,16},{12,18},{14,20},{16,22},{... | collective-permute-start | bytes 1572872 | tf_op jit(solution)/shard_map/ppermute | solution.py:21
  6.2 42.9 %collective-permute-start.1 = (bf16[256,1024]{0,1:T(8,128)(2,1)S(1)}, bf16[256,1024]{0,1:T(8,128)(2,1)}, u32[]{:S(2)}, u32[]{:S(2)}) collective-permute-start(bf16[256,1024]{0,1:T(8,128)(2,1)S(1)} %copy.234), channel_id=1, source_target_pairs={{0,4},{2,6},{4,8},{6,10},{8,12},{10,14},{12,16},{14,18},{16,20},{1... | collective-permute-start | bytes 1572872 | tf_op jit(solution)/shard_map/ppermute | solution.py:21
  10.5 33.6 %collective-permute-start = (bf16[256,1024]{0,1:T(8,128)(2,1)S(1)}, bf16[256,1024]{0,1:T(8,128)(2,1)S(1)}, u32[]{:S(2)}, u32[]{:S(2)}) collective-permute-start(bf16[256,1024]{0,1:T(8,128)(2,1)S(1)} %copy.234), channel_id=1, source_target_pairs={{0,2},{2,4},{4,6},{6,8},{8,10},{10,12},{12,14},{14,16},{16,18},{18... | collective-permute-start | bytes 1572872 | tf_op jit(solution)/shard_map/ppermute | solution.py:21
  13.6 7.3 %collective-permute-start.3 = (bf16[3,1024]{1,0:T(4,128)(2,1)S(1)}, bf16[3,1024]{1,0:T(4,128)(2,1)S(1)}, u32[]{:S(2)}, u32[]{:S(2)}) collective-permute-start(bf16[3,1024]{1,0:T(4,128)(2,1)S(1)} %slice.48), channel_id=1, source_target_pairs={{0,2},{2,4},{4,6},{6,8},{8,10},{10,12},{12,14},{14,16},{16,18},{18... | collective-permute-start | bytes 18440 | tf_op jit(solution)/shard_map/ppermute | solution.py:21
  20.7 33.2 %copy-start = (f32[8,256,256]{1,2,0:T(8,128)}, f32[8,256,256]{1,2,0:T(8,128)S(1)}, u32[]{:S(2)}) copy-start(f32[8,256,256]{1,2,0:T(8,128)S(1)} %get-tuple-element.38) | copy-start | bytes 6291460
  22.6 46.8 %collective-permute-start.5 = (bf16[256,1024]{1,0:T(8,128)(2,1)}, bf16[256,1024]{1,0:T(8,128)(2,1)}, u32[]{:S(2)}, u32[]{:S(2)}) collective-permute-start(bf16[256,1024]{1,0:T(8,128)(2,1)} %add_convert_fusion.1), channel_id=1, source_target_pairs={{0,4},{2,6},{4,8},{6,10},{8,12},{10,14},{12,16},{14,18},{16,20},{1... | collective-permute-start | bytes 1572872 | tf_op jit(solution)/shard_map/ppermute | solution.py:21
  36.4 27.9 %collective-permute-start.4 = (bf16[256,1024]{1,0:T(8,128)(2,1)}, bf16[256,1024]{1,0:T(8,128)(2,1)}, u32[]{:S(2)}, u32[]{:S(2)}) collective-permute-start(bf16[256,1024]{1,0:T(8,128)(2,1)} %add_convert_fusion.1), channel_id=1, source_target_pairs={{0,2},{2,4},{4,6},{6,8},{8,10},{10,12},{12,14},{14,16},{16,18},{18... | collective-permute-start | bytes 1572872 | tf_op jit(solution)/shard_map/ppermute | solution.py:21
  44.1 9.8 %copy-start.19 = (bf16[32,8,8,128]{3,2,1,0:T(8,128)(2,1)}, bf16[32,8,8,128]{3,2,1,0:T(8,128)(2,1)S(1)}, u32[]{:S(2)}) copy-start(bf16[32,8,8,128]{3,2,1,0:T(8,128)(2,1)S(1)} %fusion.102) | copy-start | bytes 1572868
  44.1 7.0 %copy-start.15 = (bf16[256,1024]{0,1:T(8,128)(2,1)}, bf16[256,1024]{0,1:T(8,128)(2,1)S(1)}, u32[]{:S(2)}) copy-start(bf16[256,1024]{0,1:T(8,128)(2,1)S(1)} %collective-permute-done) | copy-start | bytes 1572868
  44.2 15.3 %collective-permute-start.6 = (bf16[256,1024]{1,0:T(8,128)(2,1)}, bf16[256,1024]{1,0:T(8,128)(2,1)}, u32[]{:S(2)}, u32[]{:S(2)}) collective-permute-start(bf16[256,1024]{1,0:T(8,128)(2,1)} %add_convert_fusion.1), channel_id=1, source_target_pairs={{0,6},{2,8},{4,10},{6,12},{8,14},{10,16},{12,18},{14,20},{16,22},{... | collective-permute-start | bytes 1572872 | tf_op jit(solution)/shard_map/ppermute | solution.py:21
  74.9 6.6 %copy-start.29 = (f32[1024]{0:T(1024)S(1)}, f32[1024]{0:T(1024)}, u32[]{:S(2)}) copy-start(f32[1024]{0:T(1024)} %param.12) | copy-start | bytes 12292
  91.7 4.9 %copy-start.16 = (bf16[256,1024]{0,1:T(8,128)(2,1)}, bf16[256,1024]{0,1:T(8,128)(2,1)S(1)}, u32[]{:S(2)}) copy-start(bf16[256,1024]{0,1:T(8,128)(2,1)S(1)} %copy.165) | copy-start | bytes 1572868
  98.8 20.4 %copy-start.8 = (bf16[8,256,256]{1,2,0:T(8,128)(2,1)}, bf16[8,256,256]{1,2,0:T(8,128)(2,1)S(1)}, u32[]{:S(2)}) copy-start(bf16[8,256,256]{1,2,0:T(8,128)(2,1)S(1)} %multiply_convert_fusion.2) | copy-start | bytes 3145732
  126.1 10.9 %copy-start.9 = (bf16[8,256,256]{1,2,0:T(8,128)(2,1)S(1)}, bf16[8,256,256]{1,2,0:T(8,128)(2,1)}, u32[]{:S(2)}) copy-start(bf16[8,256,256]{1,2,0:T(8,128)(2,1)} %copy-done.8) | copy-start | bytes 3145732
  130.4 8.3 %copy-start.10 = (bf16[8,256,256]{1,2,0:T(8,128)(2,1)S(1)}, bf16[8,256,256]{1,2,0:T(8,128)(2,1)}, u32[]{:S(2)}) copy-start(bf16[8,256,256]{1,2,0:T(8,128)(2,1)} %multiply_convert_fusion) | copy-start | bytes 3145732
  130.4 8.3 %copy-start.14 = (bf16[256,1024]{0,1:T(8,128)(2,1)S(1)}, bf16[256,1024]{0,1:T(8,128)(2,1)}, u32[]{:S(2)}) copy-start(bf16[256,1024]{0,1:T(8,128)(2,1)} %copy-done.13) | copy-start | bytes 1572868
  130.4 51.1 %collective-permute-start.9 = (bf16[256,1024]{1,0:T(8,128)(2,1)}, bf16[256,1024]{1,0:T(8,128)(2,1)}, u32[]{:S(2)}, u32[]{:S(2)}) collective-permute-start(bf16[256,1024]{1,0:T(8,128)(2,1)} %copy.194), channel_id=1, source_target_pairs={{6,0},{8,2},{10,4},{12,6},{14,8},{16,10},{18,12},{20,14},{22,16},{... | collective-permute-start | bytes 1572872 | tf_op jit(solution)/shard_map/ppermute | solution.py:21
  131.8 49.7 %collective-permute-start.8 = (bf16[256,1024]{1,0:T(8,128)(2,1)}, bf16[256,1024]{1,0:T(8,128)(2,1)}, u32[]{:S(2)}, u32[]{:S(2)}) collective-permute-start(bf16[256,1024]{1,0:T(8,128)(2,1)} %copy.191), channel_id=1, source_target_pairs={{4,0},{6,2},{8,4},{10,6},{12,8},{14,10},{16,12},{18,14},{20,16},{2... | collective-permute-start | bytes 1572872 | tf_op jit(solution)/shard_map/ppermute | solution.py:21
  133.1 39.0 %collective-permute-start.12 = (bf16[256,1024]{1,0:T(8,128)(2,1)}, bf16[256,1024]{1,0:T(8,128)(2,1)S(1)}, u32[]{:S(2)}, u32[]{:S(2)}) collective-permute-start(bf16[256,1024]{1,0:T(8,128)(2,1)} %copy.202), channel_id=1, source_target_pairs={{6,0},{8,2},{10,4},{12,6},{14,8},{16,10},{18,12},{20,14},{22,16},{... | collective-permute-start | bytes 1572872 | tf_op jit(solution)/shard_map/ppermute | solution.py:21
  134.4 43.4 %collective-permute-start.11 = (bf16[256,1024]{1,0:T(8,128)(2,1)}, bf16[256,1024]{1,0:T(8,128)(2,1)}, u32[]{:S(2)}, u32[]{:S(2)}) collective-permute-start(bf16[256,1024]{1,0:T(8,128)(2,1)} %copy.200), channel_id=1, source_target_pairs={{4,0},{6,2},{8,4},{10,6},{12,8},{14,10},{16,12},{18,14},{20,16},{2... | collective-permute-start | bytes 1572872 | tf_op jit(solution)/shard_map/ppermute | solution.py:21
  135.7 42.1 %collective-permute-start.10 = (bf16[256,1024]{1,0:T(8,128)(2,1)}, bf16[256,1024]{1,0:T(8,128)(2,1)}, u32[]{:S(2)}, u32[]{:S(2)}) collective-permute-start(bf16[256,1024]{1,0:T(8,128)(2,1)} %copy.197), channel_id=1, source_target_pairs={{2,0},{4,2},{6,4},{8,6},{10,8},{12,10},{14,12},{16,14},{18,16},{20... | collective-permute-start | bytes 1572872 | tf_op jit(solution)/shard_map/ppermute | solution.py:21
  138.7 34.8 %copy-start.12 = (bf16[8,256,256]{1,2,0:T(8,128)(2,1)S(1)}, bf16[8,256,256]{1,2,0:T(8,128)(2,1)}, u32[]{:S(2)}) copy-start(bf16[8,256,256]{1,2,0:T(8,128)(2,1)} %multiply_convert_fusion.1) | copy-start | bytes 3145732
  172.1 9.4 %collective-permute-start.7 = (bf16[256,1024]{1,0:T(8,128)(2,1)}, bf16[256,1024]{1,0:T(8,128)(2,1)}, u32[]{:S(2)}, u32[]{:S(2)}) collective-permute-start(bf16[256,1024]{1,0:T(8,128)(2,1)} %copy.187), channel_id=1, source_target_pairs={{2,0},{4,2},{6,4},{8,6},{10,8},{12,10},{14,12},{16,14},{18,16},{20... | collective-permute-start | bytes 1572872 | tf_op jit(solution)/shard_map/ppermute | solution.py:21
  180.2 74.7 %collective-permute-start.13 = (f32[3,1024]{1,0:T(4,128)S(1)}, f32[3,1024]{1,0:T(4,128)S(1)}, u32[]{:S(2)}, u32[]{:S(2)}) collective-permute-start(f32[3,1024]{1,0:T(4,128)S(1)} %slice.64), channel_id=1, source_target_pairs={{2,0},{4,2},{6,4},{8,6},{10,8},{12,10},{14,12},{16,14},{18,16},{20... | collective-permute-start | bytes 36872 | tf_op jit(solution)/shard_map/ppermute | solution.py:21
  (21 other events, 52.5 us)
where the time goes:
time: 258 us; the launch traced here: 256 us
  blocking collectives  81.1 us (31%)
  starting transfers between devices  48 us (19%)
  matrix products  43.5 us (17%)
  waiting for transfers between devices  36.7 us (14%)
  local copies, waits for them, and re-layouts  28.6 us (11%)
  other arithmetic  16.9 us (7%)
    psum x1, blocking collectives, body(): conv_grad = lax.psum(local_taps, 'tm')  70.9 us
    ppermute x14, starting transfers between devices, from_behind(): return lax.ppermute(block, axis, route)  48 us
    ppermute x14, waiting for transfers between devices, from_behind(): return lax.ppermute(block, axis, route)  36.7 us
    dot_general x4, matrix products, body(): jnp.einsum('htu,uhd->thd', weights, split_heads(blocks[distance][1]), pre...  13.5 us
    dot_general x4, matrix products, body(): jnp.einsum('htu,thd->uhd', prob.astype(jnp.bfloat16), heads_grad, preferr...  8.38 us
    dot_general x4, matrix products, body(): jnp.einsum('thd,uhd->htu', heads_grad, split_heads(block_values), preferr...  6.8 us
    dot_general x4, matrix products, body(): jnp.einsum('htu,thd->uhd', score_grad, heads_query, preferred_element_typ...  5.85 us
    dot_general x4, matrix products, body(): jnp.einsum('htu,uhd->thd', score_grad, split_heads(block_keys), preferred...  5.47 us
  transfers between devices with their start and end apart: 14, of which 2 were waited for; matrix products, arithmetic and copies ran while one was open for 14% of the time, Pallas kernels for 0%

commit v1 on v0

v1 whole, which is shorter than its diff:
```python
import functools

import jax
import jax.numpy as jnp
from jax import lax
from jax.experimental import pallas as pl
from jax.experimental.pallas import tpu as pltpu
from jax.sharding import PartitionSpec as P

HD = 128
BLK = 128
LOG2E = 1.4426950408889634
NEG_FILL = -1e30
NORM_EPS = 1e-06
MESH = pl.DeviceIdType.MESH
F32 = jnp.float32
BF16 = jnp.bfloat16


def dot_nt(a, b):
    return lax.dot_general(a, b, (((1,), (1,)), ((), ())), preferred_element_type=F32)


def dot_nn(a, b):
    return jnp.dot(a, b, preferred_element_type=F32)


def kernel(
    n,
    width,
    q_ref,
    k_ref,
    v_ref,
    t_ref,
    gain_ref,
    w_ref,
    bits_ref,
    pos_ref,
    dq_ref,
    dk_ref,
    dv_ref,
    dc_ref,
    kx,
    vx,
    qx,
    gx,
    stx,
    halo,
    extv,
    dvx,
    prob,
    att,
    mask,
    mask_t,
    stats,
    norm,
    norm_out,
    norm_in,
    tap_pair,
    tap_own,
    tap_all,
    send_sem,
    recv_sem,
    st_send,
    st_recv,
    misc_send,
    misc_recv,
    tap_send,
    tap_recv,
):
    rows, channels = q_ref.shape
    heads = channels // HD
    taps = w_ref.shape[0]
    win = bits_ref.shape[1]
    span = win * BLK
    total = kx.shape[1]
    me = lax.axis_index("tm")
    side = lax.axis_index("head")
    even = lax.rem(me, 2) == 0
    odd = lax.rem(me, 2) == 1
    chips = n // 2
    scale = HD ** (-0.5)
    scale2 = scale * LOG2E

    def cols(h):
        return pl.ds(pl.multiple_of(h * HD, HD), HD)

    def put(buf, lead, src, dst, count, send, recv, target):
        return pltpu.make_async_remote_copy(
            src_ref=buf.at[lead, pl.ds(src, count)],
            dst_ref=buf.at[lead, pl.ds(dst, count)],
            send_sem=send,
            recv_sem=recv,
            device_id={"tm": target},
            device_id_type=MESH,
        )

    own = total - rows

    def ahead_direct(buf, a, h):
        s, r = send_sem.at[a], recv_sem.at[a]
        return [
            (me + 2 < n, put(buf, h, own, BLK, rows, s.at[0, h], r.at[1, h], me + 2)),
            (even, put(buf, h, own, BLK + rows, rows, s.at[1, h], r.at[0, h], me + 1)),
            (
                odd & (me + 3 < n),
                put(buf, h, own + BLK, 0, BLK, s.at[1, h], r.at[2, h], me + 3),
            ),
        ]

    def ahead_relay(buf, a, h):
        s, r = send_sem.at[a], recv_sem.at[a]
        return [
            (odd & (me >= 2), put(buf, h, BLK, BLK + rows, rows, s.at[2, h], r.at[0, h], me - 1)),
            (even & (me >= 2), put(buf, h, BLK + BLK, 0, BLK, s.at[2, h], r.at[2, h], me + 1)),
        ]

    def back_direct(buf, a, h):
        s, r = send_sem.at[a], recv_sem.at[a]
        return [
            (me >= 2, put(buf, h, 0, 2 * rows, rows, s.at[0, h], r.at[1, h], me - 2)),
            (odd, put(buf, h, 0, rows, rows, s.at[1, h], r.at[0, h], me - 1)),
            (
                even & (me >= 3),
                put(buf, h, 0, 3 * rows, BLK, s.at[1, h], r.at[2, h], me - 3),
            ),
        ]

    def back_relay(buf, a, h):
        s, r = send_sem.at[a], recv_sem.at[a]
        return [
            (even & (me + 2 < n), put(buf, h, 2 * rows, rows, rows, s.at[2, h], r.at[0, h], me + 1)),
            (odd & (me + 2 < n), put(buf, h, 2 * rows, 3 * rows, BLK, s.at[2, h], r.at[2, h], me - 1)),
        ]

    def put_stat(src, dst, count, kind, slot, target):
        return pltpu.make_async_remote_copy(
            src_ref=stx.at[:, pl.ds(src, count)],
            dst_ref=stx.at[:, pl.ds(dst, count)],
            send_sem=st_send.at[kind],
            recv_sem=st_recv.at[slot],
            device_id={"tm": target},
            device_id_type=MESH,
        )

    def stat_direct():
        return [
            (me >= 2, put_stat(0, 2 * rows, rows, 0, 1, me - 2)),
            (odd, put_stat(0, rows, rows, 1, 0, me - 1)),
            (even & (me >= 3), put_stat(0, 3 * rows, BLK, 1, 2, me - 3)),
        ]

    def stat_relay():
        return [
            (even & (me + 2 < n), put_stat(2 * rows, rows, rows, 2, 0, me + 1)),
            (odd & (me + 2 < n), put_stat(2 * rows, 3 * rows, BLK, 2, 2, me - 1)),
        ]

    def start(copies):
        for ok, copy in copies:
            pl.when(ok)(copy.start)

    def sent(copies):
        for ok, copy in copies:
            pl.when(ok)(copy.wait_send)

    def got_ahead(buf, a, h, slot):
        dst, count = ((BLK + rows, rows), (BLK, rows), (0, BLK))[slot - 1]
        copy = put(buf, h, dst, dst, count, send_sem.at[a, 0, h], recv_sem.at[a, slot - 1, h], me)
        pl.when(me >= slot)(copy.wait_recv)

    def got_back(buf, a, h, slot):
        dst, count = slot * rows, BLK if slot == 3 else rows
        copy = put(buf, h, dst, dst, count, send_sem.at[a, 0, h], recv_sem.at[a, slot - 1, h], me)
        pl.when(me + slot < n)(copy.wait_recv)

    def got_stat(slot):
        dst, count = slot * rows, BLK if slot == 3 else rows
        pl.when(me + slot < n)(put_stat(dst, dst, count, 0, slot - 1, me).wait_recv)

    def each(body):
        def step(h, carry):
            body(h)
            return carry

        lax.fori_loop(0, heads, step, 0)

    barrier = pltpu.get_barrier_semaphore()

    def greet(i, carry):
        pl.semaphore_signal(
            barrier, inc=1, device_id={"tm": lax.rem(me + i, n)}, device_id_type=MESH
        )
        return carry

    lax.fori_loop(1, n, greet, 0)
    pl.semaphore_signal(barrier, inc=1, device_id={"head": 1 - side}, device_id_type=MESH)

    halo_rows = halo.shape[0]

    @functools.partial(each)
    def _(h):
        kx[h, own:total, :] = k_ref[:, cols(h)]

    pl.semaphore_wait(barrier, n)

    halo_copy = pltpu.make_async_remote_copy(
        src_ref=v_ref.at[pl.ds(rows - halo_rows, halo_rows)],
        dst_ref=halo,
        send_sem=misc_send.at[0],
        recv_sem=misc_recv.at[0],
        device_id={"tm": me + 1},
        device_id_type=MESH,
    )
    pl.when(me + 1 < n)(halo_copy.start)

    @functools.partial(each)
    def _(h):
        start(ahead_direct(kx, 0, h))

    for slot, (dst, count) in enumerate(((BLK + rows, rows), (BLK, rows), (0, BLK)), 1):

        @pl.when(me < slot)
        def _(dst=dst, count=count):
            @functools.partial(each)
            def _(h):
                kx[h, dst : dst + count, :] = jnp.zeros((count, HD), BF16)
                vx[h, dst : dst + count, :] = jnp.zeros((count, HD), BF16)

        back, back_count = slot * rows, BLK if slot == 3 else rows

        @pl.when(me + slot >= n)
        def _(dst=back, count=back_count):
            @functools.partial(each)
            def _(h):
                qx[h, dst : dst + count, :] = jnp.zeros((count, HD), BF16)
                gx[h, dst : dst + count, :] = jnp.zeros((count, HD), BF16)

            stx[:, dst : dst + count] = jnp.full((stx.shape[0], count), NEG_FILL, F32)

    @pl.when(me < 1)
    def _():
        halo[...] = jnp.zeros(halo.shape, BF16)

    pl.when(me >= 1)(halo_copy.wait_recv)

    @functools.partial(each)
    def _(h):
        extv[h, 0:8, :] = halo[:, cols(h)].astype(F32)[halo_rows - 8 :]
        extv[h, 8 : 8 + rows, :] = v_ref[:, cols(h)].astype(F32)
        acc = jnp.zeros((rows, HD), F32)
        for j in range(taps):
            acc = acc + w_ref[j : j + 1, cols(h)] * extv[h, 8 - j : 8 - j + rows, :]
        vx[h, own:total, :] = acc.astype(BF16)
        start(ahead_direct(vx, 1, h))

    @functools.partial(each)
    def _(h):
        qx[h, 0:rows, :] = q_ref[:, cols(h)]
        start(back_direct(qx, 2, h))

    line = lax.broadcasted_iota(jnp.int32, (BLK, BLK), 0)
    lane = lax.broadcasted_iota(jnp.int32, (BLK, BLK), 1)
    for i in range(rows // BLK):
        for r in range(win):
            bit = bits_ref[i, r] > 0
            there = me * (rows // BLK) + i - r >= 0
            part = jnp.full((BLK, BLK), jnp.where(bit & there, 0.0, NEG_FILL), F32)
            if r == 0:
                part = jnp.where(lane <= line, part, NEG_FILL)
            mask[i, :, (win - 1 - r) * BLK : (win - r) * BLK] = part
            stx[3 * heads + r : 3 * heads + r + 1, i * BLK : (i + 1) * BLK] = jnp.full(
                (1, BLK), jnp.where(bit, 0.0, NEG_FILL), F32
            )

    stats[...] = jnp.zeros(stats.shape, F32)
    norm[...] = jnp.zeros(norm.shape, F32)

    def relay_kv(h):
        got_ahead(kx, 0, h, 2)
        start(ahead_relay(kx, 0, h))
        got_ahead(vx, 1, h, 2)
        start(ahead_relay(vx, 1, h))

    relay_kv(0)

    @functools.partial(each)
    def _(h):
        pl.when(h + 1 < heads)(lambda: relay_kv(h + 1))
        got_ahead(kx, 0, h, 1)
        got_ahead(kx, 0, h, 3)
        got_ahead(vx, 1, h, 1)
        got_ahead(vx, 1, h, 3)
        gain = gain_ref[:, cols(h)]
        for i in range(rows // BLK):
            here = slice(i * BLK, (i + 1) * BLK)
            window = slice(i * BLK, i * BLK + span)
            s = dot_nt(qx[h, here, :], kx[h, window, :]) * scale2 + mask[i]
            peak = jnp.max(s, axis=1, keepdims=True)
            e = jnp.exp2(s - peak)
            inv = 1.0 / jnp.sum(e, axis=1, keepdims=True)
            p = e * inv
            prob[h, i] = p
            o = dot_nn(p.astype(BF16), vx[h, window, :])
            att[h, here, :] = o
            stats[here, :] = jnp.where(
                lane == h, -peak, jnp.where(lane == heads + h, inv, stats[here, :])
            )
            og = o * gain
            norm[0, here, :] += o * o
            norm[1, here, :] += og * og
            norm[2, here, :] += og * t_ref[here, cols(h)].astype(F32)

    big_lane = lax.broadcasted_iota(jnp.int32, (rows, HD), 1)
    sums = [jnp.sum(norm[i], axis=1, keepdims=True) for i in range(3)]
    norm_out[...] = jnp.where(
        big_lane == 0, sums[0], jnp.where(big_lane == 1, sums[1], sums[2])
    )
    norm_copy = pltpu.make_async_remote_copy(
        src_ref=norm_out,
        dst_ref=norm_in,
        send_sem=misc_send.at[1],
        recv_sem=misc_recv.at[1],
        device_id={"head": 1 - side},
        device_id_type=MESH,
    )
    norm_copy.start()
    chosen = jnp.concatenate(
        [
            jnp.max(
                jnp.where(
                    pos_ref[i : i + 1, :]
                    == lax.broadcasted_iota(jnp.int32, (BLK, pos_ref.shape[1]), 0),
                    1.0,
                    0.0,
                ),
                axis=1,
                keepdims=True,
            )
            for i in range(rows // BLK)
        ],
        axis=0,
    )
    norm_copy.wait_recv()
    both = norm_out[...] + norm_in[...]
    inverse = lax.rsqrt(both[:, 0:1] / width + NORM_EPS)
    cross = chosen * (inverse * both[:, 1:2] - both[:, 2:3])
    factor = inverse * inverse * inverse * cross / width

    @functools.partial(each)
    def _(h):
        gain = gain_ref[:, cols(h)]
        o = att[h]
        scaled = (o * inverse * gain - t_ref[:, cols(h)].astype(F32)) * chosen * gain
        grad = (inverse * scaled - o * factor).astype(BF16)
        gx[h, 0:rows, :] = grad
        start(back_direct(gx, 3, h))
        delta = jnp.sum(grad.astype(F32) * o, axis=1, keepdims=True)
        stats[...] = jnp.where(big_lane == 2 * heads + h, delta, stats[...])

    stx[0 : 3 * heads, 0:rows] = stats[...].T[0 : 3 * heads]
    stx[3 * heads + win :, 0:rows] = jnp.zeros((stx.shape[0] - 3 * heads - win, rows), F32)
    start(stat_direct())

    @functools.partial(each)
    def _(h):
        got_back(qx, 2, h, 2)
        start(back_relay(qx, 2, h))
        got_back(gx, 3, h, 2)
        start(back_relay(gx, 3, h))
        for i in range(rows // BLK):
            here = slice(i * BLK, (i + 1) * BLK)
            window = slice(i * BLK, i * BLK + span)
            grad = gx[h, here, :]
            delta = jnp.sum(grad.astype(F32) * att[h, here, :], axis=1, keepdims=True)
            dp = dot_nt(grad, vx[h, window, :])
            ds = (prob[h, i] * (dp - delta)).astype(BF16)
            dq_ref[here, cols(h)] = (dot_nn(ds, kx[h, window, :]) * scale).astype(BF16)

    got_stat(2)
    start(stat_relay())
    got_stat(1)
    got_stat(3)
    for i in range(rows // BLK):
        for r in range(win):
            part = jnp.broadcast_to(
                stx[3 * heads + r : 3 * heads + r + 1, (i + r) * BLK : (i + r + 1) * BLK],
                (BLK, BLK),
            )
            if r == 0:
                part = jnp.where(line <= lane, part, NEG_FILL)
            mask_t[i, :, r * BLK : (r + 1) * BLK] = part

    @functools.partial(each)
    def _(h):
        got_back(qx, 2, h, 1)
        got_back(qx, 2, h, 3)
        got_back(gx, 3, h, 1)
        got_back(gx, 3, h, 3)
        for i in range(rows // BLK):
            here = slice(own + i * BLK, own + (i + 1) * BLK)
            out = slice(i * BLK, (i + 1) * BLK)
            window = slice(i * BLK, i * BLK + span)
            peak = stx[pl.ds(h, 1), window]
            inv = stx[pl.ds(heads + h, 1), window]
            delta = stx[pl.ds(2 * heads + h, 1), window]
            s = dot_nt(kx[h, here, :], qx[h, window, :]) * scale2 + mask_t[i]
            p = jnp.exp2(s + peak) * inv
            dvx[h, out, :] = dot_nn(p.astype(BF16), gx[h, window, :])
            dp = dot_nt(vx[h, here, :], gx[h, window, :])
            ds = (p * (dp - delta)).astype(BF16)
            dk_ref[out, cols(h)] = (dot_nn(ds, qx[h, window, :]) * scale).astype(BF16)
        for j in range(taps):
            tap_own[j : j + 1, cols(h)] = jnp.sum(
                dvx[h, 0:rows, :] * extv[h, 8 - j : 8 - j + rows, :], axis=0, keepdims=True
            )

    rim_copy = pltpu.make_async_remote_copy(
        src_ref=dvx.at[:, pl.ds(0, 8)],
        dst_ref=dvx.at[:, pl.ds(rows, 8)],
        send_sem=misc_send.at[2],
        recv_sem=misc_recv.at[2],
        device_id={"tm": me - 1},
        device_id_type=MESH,
    )
    pair_copy = pltpu.make_async_remote_copy(
        src_ref=tap_own,
        dst_ref=tap_pair,
        send_sem=misc_send.at[3],
        recv_sem=misc_recv.at[3],
        device_id={"tm": me + 1 - 2 * lax.rem(me, 2)},
        device_id_type=MESH,
    )
    pair_copy.start()
    pl.when(me >= 1)(rim_copy.start)
    core = lax.rem(me, 2)
    chip = me // 2
    pair_copy.wait_recv()
    tap_all[chip] = tap_own[...] + tap_pair[...]

    def share(k):
        return pltpu.make_async_remote_copy(
            src_ref=tap_all.at[chip],
            dst_ref=tap_all.at[chip],
            send_sem=tap_send.at[k],
            recv_sem=tap_recv.at[k],
            device_id={"tm": lax.rem(chip + k, chips) * 2 + core},
            device_id_type=MESH,
        )

    def got_share(k):
        source = lax.rem(chip + chips - k, chips)
        return pltpu.make_async_remote_copy(
            src_ref=tap_all.at[source],
            dst_ref=tap_all.at[source],
            send_sem=tap_send.at[k],
            recv_sem=tap_recv.at[k],
            device_id={"tm": me},
            device_id_type=MESH,
        )

    def run(first, last, body):
        def step(k, carry):
            body(k)
            return carry

        lax.fori_loop(first, last, step, 0)

    run(1, chips, lambda k: share(k).start())

    @pl.when(me + 1 >= n)
    def _():
        dvx[:, rows : rows + 8, :] = jnp.zeros((heads, 8, HD), F32)

    pl.when(me + 1 < n)(rim_copy.wait_recv)

    @functools.partial(each)
    def _(h):
        acc = jnp.zeros((rows, HD), F32)
        for j in range(taps):
            acc = acc + w_ref[j : j + 1, cols(h)] * dvx[h, j : j + rows, :]
        dv_ref[:, cols(h)] = acc.astype(BF16)

    @functools.partial(each)
    def _(h):
        sent(ahead_direct(kx, 0, h))
        sent(ahead_relay(kx, 0, h))
        sent(ahead_direct(vx, 1, h))
        sent(ahead_relay(vx, 1, h))
        sent(back_direct(qx, 2, h))
        sent(back_relay(qx, 2, h))
        sent(back_direct(gx, 3, h))
        sent(back_relay(gx, 3, h))

    sent(stat_direct())
    sent(stat_relay())
    pl.when(me + 1 < n)(halo_copy.wait_send)
    norm_copy.wait_send()
    pl.when(me >= 1)(rim_copy.wait_send)
    pair_copy.wait_send()
    run(1, chips, lambda k: got_share(k).wait_recv())
    acc = tap_all[0]
    for c in range(1, chips):
        acc = acc + tap_all[c]
    dc_ref[...] = acc
    run(1, chips, lambda k: share(k).wait_send())


def body(n, parts, queries, keys, values_in, teacher, gain, conv_weight, block_bits, mask_pos):
    rows, channels = queries.shape
    heads = channels // HD
    taps = conv_weight.shape[0]
    win = block_bits.shape[1]
    span = win * BLK
    total = span + rows - BLK
    blocks = rows // BLK
    stat_rows = -(-(3 * heads + win) // 8) * 8
    vmem = pl.BlockSpec(memory_space=pltpu.VMEM)
    smem = pl.BlockSpec(memory_space=pltpu.SMEM)
    dma = pltpu.SemaphoreType.DMA
    return pl.pallas_call(
        functools.partial(kernel, n, channels * parts),
        out_shape=(
            jax.ShapeDtypeStruct((rows, channels), BF16),
            jax.ShapeDtypeStruct((rows, channels), BF16),
            jax.ShapeDtypeStruct((rows, channels), BF16),
            jax.ShapeDtypeStruct((taps, channels), F32),
        ),
        in_specs=[vmem] * 6 + [smem, vmem],
        out_specs=(vmem,) * 4,
        scratch_shapes=[
            pltpu.VMEM((heads, total, HD), BF16),
            pltpu.VMEM((heads, total, HD), BF16),
            pltpu.VMEM((heads, total, HD), BF16),
            pltpu.VMEM((heads, total, HD), BF16),
            pltpu.VMEM((stat_rows, total), F32),
            pltpu.VMEM((16, channels), BF16),
            pltpu.VMEM((heads, rows + 8, HD), F32),
            pltpu.VMEM((heads, rows + 8, HD), F32),
            pltpu.VMEM((heads, blocks, BLK, span), F32),
            pltpu.VMEM((heads, rows, HD), F32),
            pltpu.VMEM((blocks, BLK, span), F32),
            pltpu.VMEM((blocks, BLK, span), F32),
            pltpu.VMEM((rows, HD), F32),
            pltpu.VMEM((3, rows, HD), F32),
            pltpu.VMEM((rows, HD), F32),
            pltpu.VMEM((rows, HD), F32),
            pltpu.VMEM((taps, channels), F32),
            pltpu.VMEM((taps, channels), F32),
            pltpu.VMEM((n // 2, taps, channels), F32),
            dma((4, 3, heads)),
            dma((4, 3, heads)),
            dma((3,)),
            dma((3,)),
            dma((4,)),
            dma((4,)),
            dma((n // 2,)),
            dma((n // 2,)),
        ],
        compiler_params=pltpu.CompilerParams(
            collective_id=0, has_side_effects=True, vmem_limit_bytes=48 * 1024 * 1024
        ),
    )(queries, keys, values_in, teacher, gain.reshape(1, channels), conv_weight, block_bits, mask_pos)


def solution(mesh):
    placed = (
        P("tm", "head"),
        P("tm", "head"),
        P("tm", "head"),
        P("tm", "head"),
        P("head"),
        P(None, "head"),
        P("tm", None),
        P("tm", None),
    )
    return jax.shard_map(
        functools.partial(body, mesh.shape["tm"], mesh.shape["head"]),
        mesh=mesh,
        in_specs=placed,
        out_specs=(P("tm", "head"), P("tm", "head"), P("tm", "head"), P(None, "head")),
        check_vma=False,
    )
```

time: 258 us -> 89.8 us (0.35)
  blocking collectives: 81.1 us -> 0 us
  Pallas kernels: 0 us -> 78.8 us
  starting transfers between devices: 48 us -> 0 us
  matrix products: 43.5 us -> 0 us
  waiting for transfers between devices: 36.7 us -> 0 us
  local copies, waits for them, and re-layouts: 28.6 us -> 9.9 us
  other arithmetic: 16.9 us -> 0 us
    psum x3 -> x0, blocking collectives: 81.1 us -> none  [the longest x1 70.9 us: body(): conv_grad = lax.psum(local_taps, 'tm')]
    pallas_call x0 -> x1, Pallas kernels: none -> 78.8 us  [body(): pl.pallas_call(functools.partial(kernel, n, channels * parts), out_shape=...]
    ppermute x14 -> x0, starting transfers between devices: 48 us -> none  [from_behind(): return lax.ppermute(block, axis, route)]
    dot_general x24 -> x0, matrix products: 43.5 us -> none  [the longest x4 13.5 us: body(): jnp.einsum('htu,uhd->thd', weights, split_heads(blocks[distance][1]), pre...]
    ppermute x14 -> x0, waiting for transfers between devices: 36.7 us -> none  [from_behind(): return lax.ppermute(block, axis, route)]
    convert_element_type x7 -> x0, local copies, waits for them, and re-layouts: 11.7 us -> none  [the longest x3 5.26 us: body(): partials[distance][0].astype(jnp.bfloat16)]
    reduce_sum x5 -> x0, other arithmetic: 8.46 us -> none  [the longest x1 2.38 us: body(): jnp.sum(value_acc * extended[rim_rows - tap_index:rim_rows - tap_index +...]
    reshape x5 -> x0, local copies, waits for them, and re-layouts: 8.15 us -> none  [the longest x1 2.54 us: body(): value_part.reshape(row_count, channels)]
  transfers between devices with their start and end apart: 14 -> 0, of which waited for: 2 -> 0; matrix products, arithmetic and copies ran while one was open for 14% -> 0% of each run, Pallas kernels for 0% -> 0%
where the time goes in v1:
time: 89.8 us; the launch traced here: 89.4 us
  Pallas kernels  78.8 us (88%)
  local copies, waits for them, and re-layouts  9.9 us (11%)
    pallas_call x1, Pallas kernels, body(): pl.pallas_call(functools.partial(kernel, n, channels * parts), out_shape=...  78.8 us
    unnamed x20, local copies, waits for them, and re-layouts  9.9 us

profile of v1, /device:TPU:0, one launch (start us, length us, event | category | flops | bytes accessed | tf_op | source)
XLA Modules:
  0.0 89.4 jit_solution(9674748912309920543)
XLA Ops:
  0.6 0.0 copy-start.6
  0.6 0.7 copy-done.6
  1.3 0.0 copy-start
  1.3 1.0 %copy-done = bf16[256,1024]{1,0:T(8,128)(2,1)S(1)} copy-done((bf16[256,1024]{1,0:T(8,128)(2,1)S(1)}, bf16[256,1024]{1,0:T(8,128)(2,1)}, u32[]{:S(2)}) %copy-start) | copy-done | bytes 524312
  2.4 0.0 copy-start.1
  2.4 1.0 %copy-done.1 = bf16[256,1024]{1,0:T(8,128)(2,1)S(1)} copy-done((bf16[256,1024]{1,0:T(8,128)(2,1)S(1)}, bf16[256,1024]{1,0:T(8,128)(2,1)}, u32[]{:S(2)}) %copy-start.1) | copy-done | bytes 524312
  3.4 0.0 copy-start.2
  3.4 1.0 %copy-done.2 = bf16[256,1024]{1,0:T(8,128)(2,1)S(1)} copy-done((bf16[256,1024]{1,0:T(8,128)(2,1)S(1)}, bf16[256,1024]{1,0:T(8,128)(2,1)}, u32[]{:S(2)}) %copy-start.2) | copy-done | bytes 524312
  4.4 0.0 copy-start.3
  4.4 1.0 %copy-done.3 = bf16[256,1024]{1,0:T(8,128)(2,1)S(1)} copy-done((bf16[256,1024]{1,0:T(8,128)(2,1)S(1)}, bf16[256,1024]{1,0:T(8,128)(2,1)}, u32[]{:S(2)}) %copy-start.3) | copy-done | bytes 524312
  5.5 0.0 copy-start.4
  5.5 0.7 copy-done.4
  6.2 0.0 copy-start.5
  6.2 0.7 copy-done.5
  6.9 0.0 copy-start.7
  6.9 0.7 copy-done.7
  7.6 78.8 %shard_map.111 = (bf16[256,1024]{1,0:T(8,128)(2,1)S(1)}, bf16[256,1024]{1,0:T(8,128)(2,1)S(1)}, bf16[256,1024]{1,0:T(8,128)(2,1)S(1)}, f32[4,1024]{1,0:T(4,128)S(1)}) custom-call(bf16[256,1024]{1,0:T(8,128)(2,1)S(1)} %copy-done, bf16[256,1024]{1,0:T(8,128)(2,1)S(1)} %copy-done.1, bf16[256,1024]{1,0:T(8,128)(2,1)S(1)} %copy-done.2, ...), custom_call_target="tpu_custom_call" | custom-call | tf_op jit(solution)/shard_map/pallas_call | solution.py:521
  86.4 0.8 copy.16
  87.2 0.8 copy.17
  88.0 0.8 copy.18
  88.8 0.6 copy.19
Async XLA Ops:
  0.6 0.7 copy-start.6
  1.3 1.0 %copy-start = (bf16[256,1024]{1,0:T(8,128)(2,1)S(1)}, bf16[256,1024]{1,0:T(8,128)(2,1)}, u32[]{:S(2)}) copy-start(bf16[256,1024]{1,0:T(8,128)(2,1)} %q_ref.1) | copy-start | bytes 1572868
  2.4 1.0 %copy-start.1 = (bf16[256,1024]{1,0:T(8,128)(2,1)S(1)}, bf16[256,1024]{1,0:T(8,128)(2,1)}, u32[]{:S(2)}) copy-start(bf16[256,1024]{1,0:T(8,128)(2,1)} %k_ref.1) | copy-start | bytes 1572868
  3.4 1.0 %copy-start.2 = (bf16[256,1024]{1,0:T(8,128)(2,1)S(1)}, bf16[256,1024]{1,0:T(8,128)(2,1)}, u32[]{:S(2)}) copy-start(bf16[256,1024]{1,0:T(8,128)(2,1)} %v_ref.1) | copy-start | bytes 1572868
  4.4 1.0 %copy-start.3 = (bf16[256,1024]{1,0:T(8,128)(2,1)S(1)}, bf16[256,1024]{1,0:T(8,128)(2,1)}, u32[]{:S(2)}) copy-start(bf16[256,1024]{1,0:T(8,128)(2,1)} %t_ref.1) | copy-start | bytes 1572868
  5.5 0.7 copy-start.4
  6.2 0.7 copy-start.5
  6.9 0.7 copy-start.7

commit v2 on v1

--- a/solution.py
+++ b/solution.py
@@ -28,18 +28,23 @@
 def kernel(
     n,
     width,
-    q_ref,
-    k_ref,
+    q_hbm,
+    k_hbm,
+    v_hbm,
+    t_hbm,
+    gain_hbm,
+    w_hbm,
+    bits_ref,
+    pos_hbm,
+    dq_ref,
+    dk_ref,
+    dv_ref,
+    dc_ref,
     v_ref,
     t_ref,
     gain_ref,
     w_ref,
-    bits_ref,
     pos_ref,
-    dq_ref,
-    dk_ref,
-    dv_ref,
-    dc_ref,
     kx,
     vx,
     qx,
@@ -67,8 +72,10 @@
     misc_recv,
     tap_send,
     tap_recv,
+    head_sem,
+    in_sem,
 ):
-    rows, channels = q_ref.shape
+    rows, channels = q_hbm.shape
     heads = channels // HD
     taps = w_ref.shape[0]
     win = bits_ref.shape[1]
@@ -198,10 +205,34 @@
 
     halo_rows = halo.shape[0]
 
-    @functools.partial(each)
-    def _(h):
-        kx[h, own:total, :] = k_ref[:, cols(h)]
-
+    def load_key(h):
+        return pltpu.make_async_copy(
+            k_hbm.at[:, cols(h)], kx.at[h, pl.ds(own, rows)], head_sem.at[0, h]
+        )
+
+    def load_query(h):
+        return pltpu.make_async_copy(
+            q_hbm.at[:, cols(h)], qx.at[h, pl.ds(0, rows)], head_sem.at[1, h]
+        )
+
+    loads = [
+        pltpu.make_async_copy(a, b, in_sem.at[i])
+        for i, (a, b) in enumerate(
+            (
+                (v_hbm, v_ref),
+                (w_hbm, w_ref),
+                (gain_hbm, gain_ref),
+                (pos_hbm, pos_ref),
+                (t_hbm, t_ref),
+            )
+        )
+    ]
+    loads[0].start()
+    each(lambda h: load_key(h).start())
+    for load in loads[1:]:
+        load.start()
+    each(lambda h: load_query(h).start())
+    loads[0].wait()
     pl.semaphore_wait(barrier, n)
 
     halo_copy = pltpu.make_async_remote_copy(
@@ -214,9 +245,15 @@
     )
     pl.when(me + 1 < n)(halo_copy.start)
 
-    @functools.partial(each)
-    def _(h):
-        start(ahead_direct(kx, 0, h))
+    first = heads // 2
+
+    @functools.partial(each)
+    def _(h):
+        load_key(h).wait()
+        pl.when(h < first)(lambda: start(ahead_direct(kx, 0, h)))
+
+    for load in loads[1:]:
+        load.wait()
 
     for slot, (dst, count) in enumerate(((BLK + rows, rows), (BLK, rows), (0, BLK)), 1):
 
@@ -253,11 +290,9 @@
             acc = acc + w_ref[j : j + 1, cols(h)] * extv[h, 8 - j : 8 - j + rows, :]
         vx[h, own:total, :] = acc.astype(BF16)
         start(ahead_direct(vx, 1, h))
-
-    @functools.partial(each)
-    def _(h):
-        qx[h, 0:rows, :] = q_ref[:, cols(h)]
-        start(back_direct(qx, 2, h))
+        pl.when(h + first < heads)(lambda: start(ahead_direct(kx, 0, h + first)))
+
+    each(lambda h: load_query(h).wait())
 
     line = lax.broadcasted_iota(jnp.int32, (BLK, BLK), 0)
     lane = lax.broadcasted_iota(jnp.int32, (BLK, BLK), 1)
@@ -291,6 +326,12 @@
         got_ahead(kx, 0, h, 3)
         got_ahead(vx, 1, h, 1)
         got_ahead(vx, 1, h, 3)
+
+        @pl.when(h >= first)
+        def _():
+            start(back_direct(qx, 2, 2 * (h - first)))
+            start(back_direct(qx, 2, 2 * (h - first) + 1))
+
         gain = gain_ref[:, cols(h)]
         for i in range(rows // BLK):
             here = slice(i * BLK, (i + 1) * BLK)
@@ -354,20 +395,16 @@
         scaled = (o * inverse * gain - t_ref[:, cols(h)].astype(F32)) * chosen * gain
         grad = (inverse * scaled - o * factor).astype(BF16)
         gx[h, 0:rows, :] = grad
-        start(back_direct(gx, 3, h))
         delta = jnp.sum(grad.astype(F32) * o, axis=1, keepdims=True)
         stats[...] = jnp.where(big_lane == 2 * heads + h, delta, stats[...])
 
     stx[0 : 3 * heads, 0:rows] = stats[...].T[0 : 3 * heads]
     stx[3 * heads + win :, 0:rows] = jnp.zeros((stx.shape[0] - 3 * heads - win, rows), F32)
     start(stat_direct())
-
-    @functools.partial(each)
-    def _(h):
-        got_back(qx, 2, h, 2)
-        start(back_relay(qx, 2, h))
-        got_back(gx, 3, h, 2)
-        start(back_relay(gx, 3, h))
+    each(lambda h: start(back_direct(gx, 3, h)))
+
+    @functools.partial(each)
+    def _(h):
         for i in range(rows // BLK):
             here = slice(i * BLK, (i + 1) * BLK)
             window = slice(i * BLK, i * BLK + span)
@@ -377,8 +414,15 @@
             ds = (prob[h, i] * (dp - delta)).astype(BF16)
             dq_ref[here, cols(h)] = (dot_nn(ds, kx[h, window, :]) * scale).astype(BF16)
 
+    def relay_qg(h):
+        got_back(qx, 2, h, 2)
+        start(back_relay(qx, 2, h))
+        got_back(gx, 3, h, 2)
+        start(back_relay(gx, 3, h))
+
     got_stat(2)
     start(stat_relay())
+    relay_qg(0)
     got_stat(1)
     got_stat(3)
     for i in range(rows // BLK):
@@ -393,6 +437,7 @@
 
     @functools.partial(each)
     def _(h):
+        pl.when(h + 1 < heads)(lambda: relay_qg(h + 1))
         got_back(qx, 2, h, 1)
         got_back(qx, 2, h, 3)
         got_back(gx, 3, h, 1)
@@ -516,6 +561,7 @@
     blocks = rows // BLK
     stat_rows = -(-(3 * heads + win) // 8) * 8
     vmem = pl.BlockSpec(memory_space=pltpu.VMEM)
+    hbm = pl.BlockSpec(memory_space=pl.ANY)
     smem = pl.BlockSpec(memory_space=pltpu.SMEM)
     dma = pltpu.SemaphoreType.DMA
     return pl.pallas_call(
@@ -526,9 +572,14 @@
             jax.ShapeDtypeStruct((rows, channels), BF16),
             jax.ShapeDtypeStruct((taps, channels), F32),
         ),
-        in_specs=[vmem] * 6 + [smem, vmem],
+        in_specs=[hbm] * 6 + [smem, hbm],
         out_specs=(vmem,) * 4,
         scratch_shapes=[
+            pltpu.VMEM((rows, channels), BF16),
+            pltpu.VMEM((rows, channels), BF16),
+            pltpu.VMEM((1, channels), F32),
+            pltpu.VMEM((taps, channels), F32),
+            pltpu.VMEM(mask_pos.shape, jnp.int32),
             pltpu.VMEM((heads, total, HD), BF16),
             pltpu.VMEM((heads, total, HD), BF16),
             pltpu.VMEM((heads, total, HD), BF16),
@@ -556,9 +607,11 @@
             dma((4,)),
             dma((n // 2,)),
             dma((n // 2,)),
+            dma((2, heads)),
+            dma((5,)),
         ],
         compiler_params=pltpu.CompilerParams(
-            collective_id=0, has_side_effects=True, vmem_limit_bytes=48 * 1024 * 1024
+            collective_id=0, has_side_effects=True, vmem_limit_bytes=62 * 1024 * 1024
         ),
     )(queries, keys, values_in, teacher, gain.reshape(1, channels), conv_weight, block_bits, mask_pos)
 

time: 89.8 us -> 81.3 us (0.905)
  local copies, waits for them, and re-layouts: 9.9 us -> 4.56 us
  Pallas kernels: 78.8 us -> 75.9 us
    unnamed x20 -> x10, local copies, waits for them, and re-layouts: 9.9 us -> 4.56 us
    pallas_call x1, Pallas kernels: 78.8 us -> 75.9 us  [body(): pl.pallas_call(functools.partial(kernel, n, channels * parts), out_shape=...]
where the time goes in v2:
time: 81.3 us; the launch traced here: 81.1 us
  Pallas kernels  75.9 us (93%)
  local copies, waits for them, and re-layouts  4.56 us (6%)
    pallas_call x1, Pallas kernels, body(): pl.pallas_call(functools.partial(kernel, n, channels * parts), out_shape=...  75.9 us
    unnamed x10, local copies, waits for them, and re-layouts  4.56 us

profile of v2, /device:TPU:0, one launch (start us, length us, event | category | flops | bytes accessed | tf_op | source)
XLA Modules:
  0.0 81.1 jit_solution(7297398591658557729)
XLA Ops:
  0.6 75.9 %shard_map.111 = (bf16[256,1024]{1,0:T(8,128)(2,1)}, bf16[256,1024]{1,0:T(8,128)(2,1)}, bf16[256,1024]{1,0:T(8,128)(2,1)}, f32[4,1024]{1,0:T(4,128)}) custom-call(bf16[256,1024]{1,0:T(8,128)(2,1)} %q_hbm.1, bf16[256,1024]{1,0:T(8,128)(2,1)} %k_hbm.1, bf16[256,1024]{1,0:T(8,128)(2,1)} %v_hbm.1, bf16[256,1024]{1,0:T(8,128)(2,1)} %t_hbm.1, f32[1,1024]{1,0:T(1,128)} %bitcast.1, ...), custom_call_target="tpu_custom_call" | custom-call | tf_op jit(solution)/shard_map/pallas_call | solution.py:567
  76.5 0.0 copy-start.1
  76.5 1.9 %copy.16 = bf16[256,1024]{1,0:T(8,128)(2,1)} copy(bf16[256,1024]{1,0:T(8,128)(2,1)} %get-tuple-element.8) | data formatting | bytes 1048576
  78.5 0.0 copy-done.1
  78.5 0.0 copy-start
  78.5 0.8 copy.17
  79.3 0.4 copy-done
  79.7 0.0 copy-start.2
  79.7 0.8 copy.18
  80.5 0.0 copy-done.2
  80.5 0.6 copy.19
Async XLA Ops:
  76.5 1.9 %copy-start.1 = (bf16[256,1024]{1,0:T(8,128)(2,1)S(1)}, bf16[256,1024]{1,0:T(8,128)(2,1)}, u32[]{:S(2)}) copy-start(bf16[256,1024]{1,0:T(8,128)(2,1)} %get-tuple-element.9) | copy-start | bytes 1572868
  78.5 1.2 %copy-start = (bf16[256,1024]{1,0:T(8,128)(2,1)S(1)}, bf16[256,1024]{1,0:T(8,128)(2,1)}, u32[]{:S(2)}) copy-start(bf16[256,1024]{1,0:T(8,128)(2,1)} %get-tuple-element.10) | copy-start | bytes 1572868
  79.7 0.8 copy-start.2

commit v3 on v2

--- a/solution.py
+++ b/solution.py
@@ -192,6 +192,13 @@
 
         lax.fori_loop(0, heads, step, 0)
 
+    def each_pair(body):
+        def step(g, carry):
+            body((2 * g, 2 * g + 1))
+            return carry
+
+        lax.fori_loop(0, heads // 2, step, 0)
+
     barrier = pltpu.get_barrier_semaphore()
 
     def greet(i, carry):
@@ -308,6 +315,11 @@
                 (1, BLK), jnp.where(bit, 0.0, NEG_FILL), F32
             )
 
+    @functools.partial(each)
+    def _(h):
+        prob[h, 0:BLK, span:total] = jnp.zeros((BLK, total - span), F32)
+        prob[h, rows - BLK : rows, 0 : rows - BLK] = jnp.zeros((BLK, rows - BLK), F32)
+
     stats[...] = jnp.zeros(stats.shape, F32)
     norm[...] = jnp.zeros(norm.shape, F32)
 
@@ -341,7 +353,7 @@
             e = jnp.exp2(s - peak)
             inv = 1.0 / jnp.sum(e, axis=1, keepdims=True)
             p = e * inv
-            prob[h, i] = p
+            prob[h, here, window] = p
             o = dot_nn(p.astype(BF16), vx[h, window, :])
             att[h, here, :] = o
             stats[here, :] = jnp.where(
@@ -403,16 +415,14 @@
     start(stat_direct())
     each(lambda h: start(back_direct(gx, 3, h)))
 
-    @functools.partial(each)
-    def _(h):
-        for i in range(rows // BLK):
-            here = slice(i * BLK, (i + 1) * BLK)
-            window = slice(i * BLK, i * BLK + span)
-            grad = gx[h, here, :]
-            delta = jnp.sum(grad.astype(F32) * att[h, here, :], axis=1, keepdims=True)
-            dp = dot_nt(grad, vx[h, window, :])
-            ds = (prob[h, i] * (dp - delta)).astype(BF16)
-            dq_ref[here, cols(h)] = (dot_nn(ds, kx[h, window, :]) * scale).astype(BF16)
+    @functools.partial(each_pair)
+    def _(pair):
+        for h in pair:
+            grad = gx[h, 0:rows, :]
+            delta = jnp.sum(grad.astype(F32) * att[h], axis=1, keepdims=True)
+            dp = dot_nt(grad, vx[h])
+            ds = (prob[h] * (dp - delta)).astype(BF16)
+            dq_ref[:, cols(h)] = (dot_nn(ds, kx[h]) * scale).astype(BF16)
 
     def relay_qg(h):
         got_back(qx, 2, h, 2)
@@ -423,8 +433,10 @@
     got_stat(2)
     start(stat_relay())
     relay_qg(0)
+    relay_qg(1)
     got_stat(1)
     got_stat(3)
+    mask_t[...] = jnp.full(mask_t.shape, NEG_FILL, F32)
     for i in range(rows // BLK):
         for r in range(win):
             part = jnp.broadcast_to(
@@ -433,32 +445,34 @@
             )
             if r == 0:
                 part = jnp.where(line <= lane, part, NEG_FILL)
-            mask_t[i, :, r * BLK : (r + 1) * BLK] = part
-
-    @functools.partial(each)
-    def _(h):
-        pl.when(h + 1 < heads)(lambda: relay_qg(h + 1))
-        got_back(qx, 2, h, 1)
-        got_back(qx, 2, h, 3)
-        got_back(gx, 3, h, 1)
-        got_back(gx, 3, h, 3)
-        for i in range(rows // BLK):
-            here = slice(own + i * BLK, own + (i + 1) * BLK)
-            out = slice(i * BLK, (i + 1) * BLK)
-            window = slice(i * BLK, i * BLK + span)
-            peak = stx[pl.ds(h, 1), window]
-            inv = stx[pl.ds(heads + h, 1), window]
-            delta = stx[pl.ds(2 * heads + h, 1), window]
-            s = dot_nt(kx[h, here, :], qx[h, window, :]) * scale2 + mask_t[i]
+            mask_t[i * BLK : (i + 1) * BLK, (i + r) * BLK : (i + r + 1) * BLK] = part
+
+    @functools.partial(each_pair)
+    def _(pair):
+        @pl.when(pair[1] + 1 < heads)
+        def _():
+            relay_qg(pair[1] + 1)
+            relay_qg(pair[1] + 2)
+
+        for h in pair:
+            for slot in (1, 3):
+                got_back(qx, 2, h, slot)
+                got_back(gx, 3, h, slot)
+        for h in pair:
+            peak = stx[pl.ds(h, 1), :]
+            inv = stx[pl.ds(heads + h, 1), :]
+            delta = stx[pl.ds(2 * heads + h, 1), :]
+            s = dot_nt(kx[h, own:total, :], qx[h]) * scale2 + mask_t[...]
             p = jnp.exp2(s + peak) * inv
-            dvx[h, out, :] = dot_nn(p.astype(BF16), gx[h, window, :])
-            dp = dot_nt(vx[h, here, :], gx[h, window, :])
+            dvx[h, 0:rows, :] = dot_nn(p.astype(BF16), gx[h])
+            dp = dot_nt(vx[h, own:total, :], gx[h])
             ds = (p * (dp - delta)).astype(BF16)
-            dk_ref[out, cols(h)] = (dot_nn(ds, qx[h, window, :]) * scale).astype(BF16)
-        for j in range(taps):
-            tap_own[j : j + 1, cols(h)] = jnp.sum(
-                dvx[h, 0:rows, :] * extv[h, 8 - j : 8 - j + rows, :], axis=0, keepdims=True
-            )
+            dk_ref[:, cols(h)] = (dot_nn(ds, qx[h]) * scale).astype(BF16)
+        for h in pair:
+            for j in range(taps):
+                tap_own[j : j + 1, cols(h)] = jnp.sum(
+                    dvx[h, 0:rows, :] * extv[h, 8 - j : 8 - j + rows, :], axis=0, keepdims=True
+                )
 
     rim_copy = pltpu.make_async_remote_copy(
         src_ref=dvx.at[:, pl.ds(0, 8)],
@@ -588,10 +602,10 @@
             pltpu.VMEM((16, channels), BF16),
             pltpu.VMEM((heads, rows + 8, HD), F32),
             pltpu.VMEM((heads, rows + 8, HD), F32),
-            pltpu.VMEM((heads, blocks, BLK, span), F32),
+            pltpu.VMEM((heads, rows, total), F32),
             pltpu.VMEM((heads, rows, HD), F32),
             pltpu.VMEM((blocks, BLK, span), F32),
-            pltpu.VMEM((blocks, BLK, span), F32),
+            pltpu.VMEM((rows, total), F32),
             pltpu.VMEM((rows, HD), F32),
             pltpu.VMEM((3, rows, HD), F32),
             pltpu.VMEM((rows, HD), F32),

time: 81.3 us -> 81.6 us (level)
  no operation moved by 1% of the time
where the time goes in v3:
time: 81.6 us; the launch traced here: 81.3 us
  Pallas kernels  76.1 us (93%)
  local copies, waits for them, and re-layouts  4.56 us (6%)
    pallas_call x1, Pallas kernels, body(): pl.pallas_call(functools.partial(kernel, n, channels * parts), out_shape=...  76.1 us
    unnamed x10, local copies, waits for them, and re-layouts  4.56 us

profile of v3, /device:TPU:0, one launch (start us, length us, event | category | flops | bytes accessed | tf_op | source)
XLA Modules:
  0.0 81.3 jit_solution(11426068773297511483)
XLA Ops:
  0.6 76.1 %shard_map.111 = (bf16[256,1024]{1,0:T(8,128)(2,1)}, bf16[256,1024]{1,0:T(8,128)(2,1)}, bf16[256,1024]{1,0:T(8,128)(2,1)}, f32[4,1024]{1,0:T(4,128)}) custom-call(bf16[256,1024]{1,0:T(8,128)(2,1)} %q_hbm.1, bf16[256,1024]{1,0:T(8,128)(2,1)} %k_hbm.1, bf16[256,1024]{1,0:T(8,128)(2,1)} %v_hbm.1, bf16[256,1024]{1,0:T(8,128)(2,1)} %t_hbm.1, f32[1,1024]{1,0:T(1,128)} %bitcast.1, ...), custom_call_target="tpu_custom_call" | custom-call | tf_op jit(solution)/shard_map/pallas_call | solution.py:581
  76.8 0.0 copy-start.1
  76.8 1.9 %copy.16 = bf16[256,1024]{1,0:T(8,128)(2,1)} copy(bf16[256,1024]{1,0:T(8,128)(2,1)} %get-tuple-element.8) | data formatting | bytes 1048576
  78.7 0.0 copy-done.1
  78.7 0.0 copy-start
  78.7 0.8 copy.17
  79.5 0.4 copy-done
  79.9 0.0 copy-start.2
  79.9 0.8 copy.18
  80.7 0.0 copy-done.2
  80.7 0.6 copy.19
Async XLA Ops:
  76.8 1.9 %copy-start.1 = (bf16[256,1024]{1,0:T(8,128)(2,1)S(1)}, bf16[256,1024]{1,0:T(8,128)(2,1)}, u32[]{:S(2)}) copy-start(bf16[256,1024]{1,0:T(8,128)(2,1)} %get-tuple-element.9) | copy-start | bytes 1572868
  78.7 1.2 %copy-start = (bf16[256,1024]{1,0:T(8,128)(2,1)S(1)}, bf16[256,1024]{1,0:T(8,128)(2,1)}, u32[]{:S(2)}) copy-start(bf16[256,1024]{1,0:T(8,128)(2,1)} %get-tuple-element.10) | copy-start | bytes 1572868
  79.9 0.8 copy-start.2

commit v4 on v2

--- a/solution.py
+++ b/solution.py
@@ -327,11 +327,7 @@
         got_ahead(vx, 1, h, 1)
         got_ahead(vx, 1, h, 3)
 
-        @pl.when(h >= first)
-        def _():
-            start(back_direct(qx, 2, 2 * (h - first)))
-            start(back_direct(qx, 2, 2 * (h - first) + 1))
-
+        start(back_direct(qx, 2, h))
         gain = gain_ref[:, cols(h)]
         for i in range(rows // BLK):
             here = slice(i * BLK, (i + 1) * BLK)

time: 81.3 us -> 78.1 us (0.961)
  Pallas kernels: 75.9 us -> 72.7 us
    pallas_call x1, Pallas kernels: 75.9 us -> 72.7 us  [body(): pl.pallas_call(functools.partial(kernel, n, channels * parts), out_shape=...]
where the time goes in v4:
time: 78.1 us; the launch traced here: 77.9 us
  Pallas kernels  72.7 us (93%)
  local copies, waits for them, and re-layouts  4.56 us (6%)
    pallas_call x1, Pallas kernels, body(): pl.pallas_call(functools.partial(kernel, n, channels * parts), out_shape=...  72.7 us
    unnamed x10, local copies, waits for them, and re-layouts  4.56 us

profile of v4, /device:TPU:0, one launch (start us, length us, event | category | flops | bytes accessed | tf_op | source)
XLA Modules:
  0.0 77.9 jit_solution(10034441364933658491)
XLA Ops:
  0.6 72.7 %shard_map.111 = (bf16[256,1024]{1,0:T(8,128)(2,1)}, bf16[256,1024]{1,0:T(8,128)(2,1)}, bf16[256,1024]{1,0:T(8,128)(2,1)}, f32[4,1024]{1,0:T(4,128)}) custom-call(bf16[256,1024]{1,0:T(8,128)(2,1)} %q_hbm.1, bf16[256,1024]{1,0:T(8,128)(2,1)} %k_hbm.1, bf16[256,1024]{1,0:T(8,128)(2,1)} %v_hbm.1, bf16[256,1024]{1,0:T(8,128)(2,1)} %t_hbm.1, f32[1,1024]{1,0:T(1,128)} %bitcast.1, ...), custom_call_target="tpu_custom_call" | custom-call | tf_op jit(solution)/shard_map/pallas_call | solution.py:563
  73.3 0.0 copy-start.1
  73.3 1.9 %copy.16 = bf16[256,1024]{1,0:T(8,128)(2,1)} copy(bf16[256,1024]{1,0:T(8,128)(2,1)} %get-tuple-element.8) | data formatting | bytes 1048576
  75.3 0.0 copy-done.1
  75.3 0.0 copy-start
  75.3 0.8 %copy.17 = bf16[256,1024]{1,0:T(8,128)(2,1)} copy(bf16[256,1024]{1,0:T(8,128)(2,1)S(1)} %copy-done.1) | data formatting | bytes 1048576
  76.1 0.4 copy-done
  76.5 0.0 copy-start.2
  76.5 0.8 %copy.18 = bf16[256,1024]{1,0:T(8,128)(2,1)} copy(bf16[256,1024]{1,0:T(8,128)(2,1)S(1)} %copy-done) | data formatting | bytes 1048576
  77.3 0.0 copy-done.2
  77.3 0.6 copy.19
Async XLA Ops:
  73.3 1.9 %copy-start.1 = (bf16[256,1024]{1,0:T(8,128)(2,1)S(1)}, bf16[256,1024]{1,0:T(8,128)(2,1)}, u32[]{:S(2)}) copy-start(bf16[256,1024]{1,0:T(8,128)(2,1)} %get-tuple-element.9) | copy-start | bytes 1572868
  75.3 1.2 %copy-start = (bf16[256,1024]{1,0:T(8,128)(2,1)S(1)}, bf16[256,1024]{1,0:T(8,128)(2,1)}, u32[]{:S(2)}) copy-start(bf16[256,1024]{1,0:T(8,128)(2,1)} %get-tuple-element.10) | copy-start | bytes 1572868
  76.5 0.8 %copy-start.2 = (f32[4,1024]{1,0:T(4,128)S(1)}, f32[4,1024]{1,0:T(4,128)}, u32[]{:S(2)}) copy-start(f32[4,1024]{1,0:T(4,128)} %get-tuple-element.11) | copy-start | bytes 49156
